TPU v7x, 128 devices: a whole 4x4x4 slice. The times are simulated.
128 devices in a mesh: tile: 64 (over y, z, x), chan: 2 (over core).
Axes of the slice: x: 4, y: 4, z: 4, core: 2. Of those that a mesh axis runs over, the one named last changes fastest.
Arguments:
- attributes: bfloat16 [35, 1024, 512], P(None, 'tile'), may hold values from -6 to 6
- cell_basin: int32 [1024, 512], P('tile'), may hold values from 0 to 8191, as said below
- basin_cells: int32 [8192], P('tile'), may hold values from 1 to 127, as said below
- conv_first: bfloat16 [128, 3, 3, 35], P('chan'), may hold values from -0.5 to 0.5
- conv_second: bfloat16 [128, 3, 3, 128], P('chan'), may hold values from -0.25 to 0.25
- conv_third: bfloat16 [128, 3, 3, 128], P('chan'), may hold values from -0.25 to 0.25
- head_weight: bfloat16 [128, 12], P('chan'), may hold values from -0.75 to 0.75
- precip: float32 [30, 16, 8192], P(None, 'chan', 'tile'), may hold values from 0 to 250
- temp: float32 [30, 16, 8192], P(None, 'chan', 'tile'), may hold values from -24 to 24
- pet: float32 [30, 16, 8192], P(None, 'chan', 'tile'), may hold values from 0.5 to 4
Outputs:
- streamflow: float32 [30, 16, 8192], P(None, 'chan', 'tile')
Inputs may be any that keep to these rules, and one draw needn't show every extreme that they name: `cell_basin`: in each tile the 8192 cells in row-major order form 64 runs of 128 cells; the runs of one tile go to 64 different owners, so that every owner receives exactly 128 cells from every tile. The basins of owner o are o * 128 to o * 128 + 127; one run holds 2 whole basins, each a contiguous part of the run. `basin_cells`: the number of cells of cell_basin in each basin; some basin reaches the most.
All inputs are finite; a program needn't handle non-finite values.
Results may differ from a plain program's by a relative error of at most 0.00061.
Values may be sent and summed in bfloat16 or wider, within the bound.
A program may use at most 64 MiB of HBM per device.

v0:
```python
import jax
import jax.numpy as jnp
from jax import lax
from jax.sharding import PartitionSpec as P

LAGS = 15
LOW = [-2.0, 0.5, 50.0, 1.0, 0.3, 0.05, 0.01, 0.001, 0.0, 0.5, 1.0, 0.5]
SPAN = [4.0, 5.5, 450.0, 4.0, 0.7, 0.45, 0.29, 0.099, 50.0, 5.5, 2.0, 2.5]


def padded_2(cells, sides, width):
    for axis, dim in sides:
        count = lax.axis_size(axis)
        ends = count - 1
        head = lax.slice_in_dim(cells, 0, width, axis=dim)
        tail = lax.slice_in_dim(cells, cells.shape[dim] - width, cells.shape[dim], axis=dim)
        cells = jnp.concatenate(
            [
                lax.ppermute(tail, axis, [(i, (i + 1) % count) for i in range(ends)]),
                cells,
                lax.ppermute(head, axis, [((i + 1) % count, i) for i in range(ends)]),
            ],
            axis=dim,
        )
    return cells


def pad_columns(field):
    return jnp.pad(field, ((0, 0), (0, 0), (1, 1)))


def conv_taps(total, weight, padded):
    height = total.shape[1]
    width = total.shape[2]
    for row_tap in range(3):
        for col_tap in range(3):
            taps = weight[:, row_tap, col_tap, :]
            window = padded[:, row_tap : row_tap + height, col_tap : col_tap + width]
            total = total + jnp.einsum(
                "oc,chw->ohw", taps, window, preferred_element_type=jnp.float32
            )
    return total


def bucket_run(param, precip, temp, pet):
    tt, cfmax, fc, beta, lp = (param[0], param[1], param[2], param[3], param[4])
    k0, k1, k2, uzl, perc = (param[5], param[6], param[7], param[8], param[9])

    def day(state, force):
        snow, soil, upper, lower = state
        rain_in, air, demand = force
        liquid = jax.nn.sigmoid(air - tt)
        gained = snow + rain_in * (1.0 - liquid)
        snow_new = jnp.maximum(gained - cfmax * jnp.maximum(air - tt, 0.0), 0.0)
        melt = gained - snow_new
        inflow = rain_in * liquid + melt
        recharge = inflow * jnp.power(soil / fc, beta)
        soil = soil + inflow - recharge
        excess = jnp.maximum(soil - fc, 0.0)
        soil = soil - excess
        soil = jnp.where(soil < lp * fc, soil * (1.0 - demand / (lp * fc)), soil - demand)
        upper = upper + recharge + excess
        upper_new = jnp.maximum(upper - perc, 0.0)
        lower = lower + upper - upper_new
        quick = k0 * jnp.maximum(upper_new - uzl, 0.0)
        slow = k1 * upper_new
        upper = upper_new - quick - slow
        base = k2 * lower
        lower = lower - base
        return ((snow_new, soil, upper, lower), quick + slow + base)

    shape = precip.shape[1:]
    start = (
        jnp.zeros(shape, jnp.float32),
        jnp.broadcast_to(0.5 * fc, shape),
        jnp.full(shape, 5.0, jnp.float32),
        jnp.full(shape, 20.0, jnp.float32),
    )
    final, runoff = lax.scan(day, start, (precip, temp, pet))
    return runoff


def route(param, runoff):
    days = runoff.shape[0]
    lag = jnp.arange(LAGS).astype(jnp.float32) + 0.5
    weight = jnp.exp(
        (param[10] - 1.0)[None, :] * jnp.log(lag)[:, None] - lag[:, None] / param[11][None, :]
    )
    weight = weight / jnp.sum(weight, axis=0, keepdims=True)
    later = jnp.arange(days)[:, None] - jnp.arange(days)[None, :]
    pick = (later[None, :, :] == jnp.arange(LAGS)[:, None, None]).astype(jnp.float32)
    matrix = jnp.einsum("kts,kb->tsb", pick, weight, precision=lax.Precision.HIGHEST)
    return jnp.einsum("tsb,swb->twb", matrix, runoff, precision=lax.Precision.HIGHEST)


def on_device(
    attributes,
    cell_basin,
    basin_cells,
    conv_first,
    conv_second,
    conv_third,
    head_weight,
    precip,
    temp,
    pet,
):
    height = attributes.shape[1]
    width = attributes.shape[2]
    n_chan = lax.axis_size("chan")
    owners = lax.axis_size("tile")
    half = height // n_chan
    rimmed = padded_2(attributes, (("tile", 1),), 1)
    empty = jnp.zeros((conv_first.shape[0], height, width), jnp.float32)
    first = conv_taps(empty, conv_first, pad_columns(rimmed))
    hidden = jnp.maximum(first, 0.0).astype(jnp.bfloat16)
    for weight in (conv_second, conv_third):
        rim = padded_2(hidden, (("tile", 1),), 1)
        total = conv_taps(
            empty, weight, pad_columns(lax.all_gather(rim, "chan", axis=0, tiled=True))
        )
        hidden = jnp.maximum(total, 0.0).astype(jnp.bfloat16)
    raw = lax.psum_scatter(
        jnp.einsum("cp,chw->hpw", head_weight, hidden, preferred_element_type=jnp.float32),
        "chan",
        scatter_dimension=0,
        tiled=True,
    )
    params_count = raw.shape[1]
    share = jnp.transpose(jax.nn.sigmoid(raw), (1, 0, 2)).reshape(params_count, -1)
    mine = lax.dynamic_slice_in_dim(cell_basin, lax.axis_index("chan") * half, half, 0).reshape(-1)
    basins_here = basin_cells.shape[0]
    sums = jax.ops.segment_sum(share.T, mine, num_segments=owners * basins_here)
    sums = sums.T.reshape(params_count, owners, basins_here)
    arrived = lax.all_to_all(sums, "tile", split_axis=1, concat_axis=1, tiled=True)
    partial_value = jnp.sum(arrived, axis=1)
    total_sum = lax.psum(partial_value, "chan")
    mean = total_sum / basin_cells.astype(jnp.float32)[None, :]
    param = jnp.array(LOW, jnp.float32)[:, None] + jnp.array(SPAN, jnp.float32)[:, None] * mean
    runoff = bucket_run(param, precip, temp, pet)
    return route(param, runoff)


def solution(mesh):
    return jax.shard_map(
        on_device,
        mesh=mesh,
        in_specs=(
            P(None, "tile", None),
            P("tile", None),
            P("tile"),
            P("chan", None, None, None),
            P("chan", None, None, None),
            P("chan", None, None, None),
            P("chan", None),
            P(None, "chan", "tile"),
            P(None, "chan", "tile"),
            P(None, "chan", "tile"),
        ),
        out_specs=P(None, "chan", "tile"),
        check_vma=False,
    )
```

profile of v0, /device:TPU:1, one launch (start us, length us, event | category | flops | bytes accessed | tf_op | source)
XLA Modules:
  0.0 255.4 jit_solution(3265855978443713015)
XLA Ops:
  6.5 1.4 copy.77
  7.9 3.9 %collective-permute-start = (bf16[35,1,512]{2,0,1:T(8,128)(2,1)S(1)}, bf16[35,1,512]{2,0,1:T(8,128)(2,1)S(1)}, u32[]{:S(2)}, u32[]{:S(2)}) collective-permute-start(bf16[35,1,512]{2,0,1:T(8,128)(2,1)S(1)} %get-tuple-element.376), channel_id=1, source_target_pairs={{0,2},{2,4},{4,6},{6,8},{8,10},{10,12},{12,14},{14,16},{16,18},{18... | collective-permute-start | bytes 107528 | tf_op jit(solution)/shard_map/ppermute | solution.py:19
  11.9 1.4 collective-permute-start.1
  13.3 1.7 fusion.113
  15.1 1.7 collective-permute-done.1
  20.9 2.4 fusion.36
  23.3 3.2 %collective-permute-start.2 = (bf16[64,1,512]{2,0,1:T(8,128)(2,1)S(1)}, bf16[64,1,512]{2,0,1:T(8,128)(2,1)S(1)}, u32[]{:S(2)}, u32[]{:S(2)}) collective-permute-start(bf16[64,1,512]{2,0,1:T(8,128)(2,1)S(1)} %get-tuple-element.374), channel_id=1, source_target_pairs={{0,2},{2,4},{4,6},{6,8},{8,10},{10,12},{12,14},{14,16},{16,18},{18... | collective-permute-start | bytes 196616 | tf_op jit(solution)/shard_map/ppermute | solution.py:19
  26.6 1.3 collective-permute-start.3
  27.9 3.7 %collective-permute-done.3 = bf16[64,1,512]{2,0,1:T(8,128)(2,1)S(1)} collective-permute-done((bf16[64,1,512]{2,0,1:T(8,128)(2,1)S(1)}, bf16[64,1,512]{2,0,1:T(8,128)(2,1)S(1)}, u32[]{:S(2)}, u32[]{:S(2)}) %collective-permute-start.3) | collective-permute-done | bytes 65568 | tf_op jit(solution)/shard_map/ppermute | solution.py:21
  31.6 1.2 pad_maximum_fusion
  33.0 24.5 %all-gather.3.cloned.1.call-done = bf16[128,18,512]{2,0,1:T(8,128)(2,1)} async-done(((bf16[64,18,512]{2,0,1:T(8,128)(2,1)}), bf16[128,18,512]{2,0,1:T(8,128)(2,1)}) %all-gather.3.cloned.1.call-update) | async-done | bytes 2359312 | tf_op jit(solution)/shard_map/all_gather | solution.py:120
  57.5 2.5 fusion.11
  60.1 0.8 fusion.12
  60.9 0.8 fusion.13
  61.6 0.8 fusion.14
  62.4 0.8 fusion.15
  64.5 1.5 fusion.40
  66.1 3.3 %collective-permute-start.4 = (bf16[64,1,512]{2,0,1:T(8,128)(2,1)S(1)}, bf16[64,1,512]{2,0,1:T(8,128)(2,1)S(1)}, u32[]{:S(2)}, u32[]{:S(2)}) collective-permute-start(bf16[64,1,512]{2,0,1:T(8,128)(2,1)S(1)} %get-tuple-element.372), channel_id=1, source_target_pairs={{0,2},{2,4},{4,6},{6,8},{8,10},{10,12},{12,14},{14,16},{16,18},{18... | collective-permute-start | bytes 196616 | tf_op jit(solution)/shard_map/ppermute | solution.py:19
  69.4 1.3 collective-permute-start.5
  70.7 3.7 %collective-permute-done.5 = bf16[64,1,512]{2,0,1:T(8,128)(2,1)S(1)} collective-permute-done((bf16[64,1,512]{2,0,1:T(8,128)(2,1)S(1)}, bf16[64,1,512]{2,0,1:T(8,128)(2,1)S(1)}, u32[]{:S(2)}, u32[]{:S(2)}) %collective-permute-start.5) | collective-permute-done | bytes 65568 | tf_op jit(solution)/shard_map/ppermute | solution.py:21
  74.4 1.2 pad_maximum_fusion.1
  75.9 19.4 %all-gather.5.cloned.1.call-done = bf16[128,18,512]{2,0,1:T(8,128)(2,1)} async-done(((bf16[64,18,512]{2,0,1:T(8,128)(2,1)}), bf16[128,18,512]{2,0,1:T(8,128)(2,1)}) %all-gather.5.cloned.1.call-update) | async-done | bytes 2359312 | tf_op jit(solution)/shard_map/all_gather | solution.py:120
  95.3 3.9 %fusion.17 = f32[16,512,64]{1,2,0:T(8,128)} fusion(bf16[128,18,512]{2,0,1:T(8,128)(2,1)} %all-gather.5.cloned.1.call-done, bf16[64,3,3,128]{3,0,2,1:T(8,128)(2,1)S(1)} %copy-done.3), kind=kOutput, calls=%fused_computation.49 | convolution fusion | flops 134217728 | bytes 4472832 | tf_op jit(solution)/shard_map/oc,chw->ohw/dot_general | solution.py:39
  99.2 2.1 fusion.18
  101.3 2.2 fusion.19
  103.4 2.2 fusion.20
  105.6 2.1 fusion.21
  107.8 1.8 fusion.23
  109.5 1.7 fusion.25
  111.3 1.7 fusion.27
  113.0 8.3 %fusion.43 = f32[16,12,512]{2,1,0:T(8,128)} fusion(bf16[128,18,512]{2,0,1:T(8,128)(2,1)S(1)} %copy-done.1, f32[16,512,64]{1,2,0:T(8,128)} %fusion.23, f32[16,512,64]{1,2,0:T(8,128)} %fusion.21, f32[16,512,64]{1,2,0:T(8,128)} %fusion.20, f32[16,512,64]{1,2,0:T(8,128)} %fusion.25, f32[16,512,64]{1,2,0:T(8,128)} %fusion.19, f32[16,512,64]{1,2,0:T(8,128)} %fusion.18, ...), kind=kOutput, calls=%fused_computation.83 | convolution fusion | flops 152043520 | bytes 19550208 | tf_op jit(solution)/shard_map/cp,chw->hpw/dot_general | solution.py:124
  121.4 12.1 %reduce-scatter.2.cloned.1.call-done = f32[8,12,512]{2,1,0:T(8,128)} async-done(((f32[16,12,512]{2,1,0:T(8,128)}), f32[8,12,512]{2,1,0:T(8,128)}) %reduce-scatter.2.cloned.1.call-update) | async-done | bytes 196624 | tf_op jit(solution)/shard_map/reduce_scatter | solution.py:123
  133.4 1.0 divide_bitcast_fusion
  135.4 30.7 %scatter_custom_fusion = f32[8192,12]{1,0:T(8,128)} fusion(s32[4096]{0:T(1024)S(1)} %bitcast.289, f32[4096,12]{1,0:T(8,128)S(1)} %copy.84, f32[]{:T(128)} %constant.50.clone.1), kind=kCustom, calls=%fused_computation.76 | custom fusion | flops 49152 | bytes 393220 | tf_op jit(solution)/shard_map/scatter-add | solution.py:133
  166.2 3.6 %copy.85 = f32[12,64,128]{2,0,1:T(8,128)} copy(f32[12,64,128]{0,2,1:T(8,128)} %bitcast.269) | data formatting | bytes 786432 | tf_op jit(solution)/shard_map/reshape | solution.py:134
  169.8 10.1 %all-to-all-start = ((f32[12,64,128]{2,0,1:T(8,128)}), f32[12,64,128]{2,0,1:T(8,128)S(1)}, u32[]{:S(2)}, u32[]{:S(2)}) async-start(f32[12,64,128]{2,0,1:T(8,128)} %copy.85), calls=%async_computation.1 | async-start | bytes 1048576 | tf_op jit(solution)/shard_map/all_to_all | solution.py:135
  180.0 12.6 %all-to-all-done = f32[12,64,128]{2,0,1:T(8,128)S(1)} async-done(((f32[12,64,128]{2,0,1:T(8,128)}), f32[12,64,128]{2,0,1:T(8,128)S(1)}, u32[]{:S(2)}, u32[]{:S(2)}) %all-to-all-start) | async-done | bytes 393248 | tf_op jit(solution)/shard_map/all_to_all | solution.py:135
  192.7 3.8 %psum.7 = f32[12,128]{1,0:T(8,128)S(1)} all-reduce(f32[12,128]{1,0:T(8,128)S(1)} %reduce_sum.18), channel_id=1, replica_groups=mesh['tile'=64,'chan'=2] {'chan'}, use_global_device_ids=true, to_apply=%region_3.4 | all-reduce | flops 1536 | bytes 12288 | tf_op jit(solution)/shard_map/psum | solution.py:137
  197.4 1.9 copy.89
  199.3 45.1 %while.21 = (s32[]{:T(128)}, f32[8,128]{1,0:T(8,128)S(1)}, f32[8,128]{1,0:T(8,128)S(1)}, f32[8,128]{1,0:T(8,128)S(1)}, f32[8,128]{1,0:T(8,128)S(1)}, /*index=5*/...) while((s32[]{:T(128)}, f32[8,128]{1,0:T(8,128)S(1)}, ...), condition=%wide.region_5.6_spmd.clone, body=%wide.region_4.5_spmd.clone.sunk | while | flops 63491 | bytes 82640 | solution.py:79
  223.3 0.8 fusion.166
  224.8 0.8 fusion.166
  226.3 0.8 fusion.166
  230.8 0.8 fusion.166
  232.3 0.8 fusion.166
  233.8 0.8 fusion.166
  244.6 3.4 %convolution_bitcast_fusion = f32[30,8,128]{0,1,2:T(8,128)S(1)} fusion(f32[30,8,128]{0,1,2:T(8,128)S(1)} %copy.88, f32[30,30,128]{1,0,2:T(8,128)S(1)} %copy.89), kind=kOutput, calls=%fused_computation.82 | convolution fusion | flops 11059200 | bytes 706560 | tf_op jit(solution)/shard_map/tsb,swb->twb/dot_general | solution.py:93
  248.0 0.9 copy.90
  (118 shorter events, 47.9 us)
Async XLA Ops:
  6.5 114.8 %copy-start = (s32[16,512]{1,0:T(8,128)S(1)}, s32[16,512]{1,0:T(8,128)}, u32[]{:S(2)}) copy-start(s32[16,512]{1,0:T(8,128)} %param.15) | copy-start | bytes 98308
  6.5 51.0 %all-gather.3.cloned.1.call-start = ((), (), s32[]{:S(2)}) async-start(), calls=%async_computation.2 | async-start | bytes 3538944 | tf_op jit(solution)/shard_map/all_gather | solution.py:120
  7.9 7.1 %collective-permute-start = (bf16[35,1,512]{2,0,1:T(8,128)(2,1)S(1)}, bf16[35,1,512]{2,0,1:T(8,128)(2,1)S(1)}, u32[]{:S(2)}, u32[]{:S(2)}) collective-permute-start(bf16[35,1,512]{2,0,1:T(8,128)(2,1)S(1)} %get-tuple-element.376), channel_id=1, source_target_pairs={{0,2},{2,4},{4,6},{6,8},{8,10},{10,12},{12,14},{14,16},{16,18},{18... | collective-permute-start | bytes 107528 | tf_op jit(solution)/shard_map/ppermute | solution.py:19
  11.9 5.4 %copy-start.5 = (bf16[64,3,3,35]{0,3,2,1:T(8,128)(2,1)S(1)}, bf16[64,3,3,35]{0,3,2,1:T(8,128)(2,1)}, u32[]{:S(2)}) copy-start(bf16[64,3,3,35]{0,3,2,1:T(8,128)(2,1)} %param.17) | copy-start | bytes 120964
  11.9 4.9 %collective-permute-start.1 = (bf16[35,1,512]{2,0,1:T(8,128)(2,1)S(1)}, bf16[35,1,512]{2,0,1:T(8,128)(2,1)S(1)}, u32[]{:S(2)}, u32[]{:S(2)}) collective-permute-start(bf16[35,1,512]{2,0,1:T(8,128)(2,1)S(1)} %get-tuple-element.377), channel_id=1, source_target_pairs={{2,0},{4,2},{6,4},{8,6},{10,8},{12,10},{14,12},{16,14},{18,16},{20... | collective-permute-start | bytes 107528 | tf_op jit(solution)/shard_map/ppermute | solution.py:21
  23.3 34.2 %copy-start.4 = (bf16[64,3,3,128]{3,0,2,1:T(8,128)(2,1)S(1)}, bf16[64,3,3,128]{3,0,2,1:T(8,128)(2,1)}, u32[]{:S(2)}) copy-start(bf16[64,3,3,128]{3,0,2,1:T(8,128)(2,1)} %param.18) | copy-start | bytes 442372
  23.3 4.6 %collective-permute-start.2 = (bf16[64,1,512]{2,0,1:T(8,128)(2,1)S(1)}, bf16[64,1,512]{2,0,1:T(8,128)(2,1)S(1)}, u32[]{:S(2)}, u32[]{:S(2)}) collective-permute-start(bf16[64,1,512]{2,0,1:T(8,128)(2,1)S(1)} %get-tuple-element.374), channel_id=1, source_target_pairs={{0,2},{2,4},{4,6},{6,8},{8,10},{10,12},{12,14},{14,16},{16,18},{18... | collective-permute-start | bytes 196616 | tf_op jit(solution)/shard_map/ppermute | solution.py:19
  26.6 5.0 %collective-permute-start.3 = (bf16[64,1,512]{2,0,1:T(8,128)(2,1)S(1)}, bf16[64,1,512]{2,0,1:T(8,128)(2,1)S(1)}, u32[]{:S(2)}, u32[]{:S(2)}) collective-permute-start(bf16[64,1,512]{2,0,1:T(8,128)(2,1)S(1)} %get-tuple-element.375), channel_id=1, source_target_pairs={{2,0},{4,2},{6,4},{8,6},{10,8},{12,10},{14,12},{16,14},{18,16},{20... | collective-permute-start | bytes 196616 | tf_op jit(solution)/shard_map/ppermute | solution.py:21
  32.8 62.5 %all-gather.5.cloned.1.call-start = ((), (), s32[]{:S(2)}) async-start(), calls=%async_computation.3 | async-start | bytes 3538944 | tf_op jit(solution)/shard_map/all_gather | solution.py:120
  57.5 2.5 copy-start.2
  66.0 29.3 %copy-start.3 = (bf16[64,3,3,128]{3,0,2,1:T(8,128)(2,1)S(1)}, bf16[64,3,3,128]{3,0,2,1:T(8,128)(2,1)}, u32[]{:S(2)}) copy-start(bf16[64,3,3,128]{3,0,2,1:T(8,128)(2,1)} %param.19) | copy-start | bytes 442372
  66.1 4.6 %collective-permute-start.4 = (bf16[64,1,512]{2,0,1:T(8,128)(2,1)S(1)}, bf16[64,1,512]{2,0,1:T(8,128)(2,1)S(1)}, u32[]{:S(2)}, u32[]{:S(2)}) collective-permute-start(bf16[64,1,512]{2,0,1:T(8,128)(2,1)S(1)} %get-tuple-element.372), channel_id=1, source_target_pairs={{0,2},{2,4},{4,6},{6,8},{8,10},{10,12},{12,14},{14,16},{16,18},{18... | collective-permute-start | bytes 196616 | tf_op jit(solution)/shard_map/ppermute | solution.py:19
  69.4 5.0 %collective-permute-start.5 = (bf16[64,1,512]{2,0,1:T(8,128)(2,1)S(1)}, bf16[64,1,512]{2,0,1:T(8,128)(2,1)S(1)}, u32[]{:S(2)}, u32[]{:S(2)}) collective-permute-start(bf16[64,1,512]{2,0,1:T(8,128)(2,1)S(1)} %get-tuple-element.373), channel_id=1, source_target_pairs={{2,0},{4,2},{6,4},{8,6},{10,8},{12,10},{14,12},{16,14},{18,16},{20... | collective-permute-start | bytes 196616 | tf_op jit(solution)/shard_map/ppermute | solution.py:21
  75.6 57.8 %reduce-scatter.2.cloned.1.call-start = ((), (), s32[]{:S(2)}) async-start(), calls=%async_computation.4 | async-start | bytes 786432 | tf_op jit(solution)/shard_map/reduce_scatter | solution.py:123
  95.3 3.9 %copy-start.1 = (bf16[128,18,512]{2,0,1:T(8,128)(2,1)S(1)}, bf16[128,18,512]{2,0,1:T(8,128)(2,1)}, u32[]{:S(2)}) copy-start(bf16[128,18,512]{2,0,1:T(8,128)(2,1)} %all-gather.5.cloned.1.call-done) | copy-start | bytes 7077892
  111.3 1.7 copy-start.6
  166.2 13.8 %copy-start.9 = (s32[128]{0:T(128)S(1)}, s32[128]{0:T(128)}, u32[]{:S(2)}) copy-start(s32[128]{0:T(128)} %param.16) | copy-start | bytes 1540
  166.2 30.4 %copy-start.7 = (f32[12]{0:T(128)S(1)}, f32[12]{0:T(128)}, u32[]{:S(2)}) copy-start(f32[12]{0:T(128)} %constant.60.clone) | copy-start | bytes 148
  166.2 30.4 %copy-start.8 = (f32[12]{0:T(128)S(1)}, f32[12]{0:T(128)}, u32[]{:S(2)}) copy-start(f32[12]{0:T(128)} %constant.61.clone) | copy-start | bytes 148
  169.8 22.9 %all-to-all-start = ((f32[12,64,128]{2,0,1:T(8,128)}), f32[12,64,128]{2,0,1:T(8,128)S(1)}, u32[]{:S(2)}, u32[]{:S(2)}) async-start(f32[12,64,128]{2,0,1:T(8,128)} %copy.85), calls=%async_computation.1 | async-start | bytes 1048576 | tf_op jit(solution)/shard_map/all_to_all | solution.py:135
Sparse Core Ops, SparseCore 0:
  32.9 24.5 all-gather.2
  75.8 19.4 all-gather.4
  121.4 11.9 reduce-scatter.1
where the time goes:
time: 259 us; the launch traced here: 255 us
  other arithmetic  79.3 us (31%)
  waiting for transfers between devices  77.8 us (30%)
  matrix products  46.1 us (18%)
  starting transfers between devices  25.1 us (10%)
  between operations  13.5 us (5%)
  local copies, waits for them, and re-layouts  9.06 us (3%)
  blocking collectives  3.81 us (1%)
    all_gather x2, waiting for transfers between devices, on_device(): lax.all_gather(rim, 'chan', axis=0, tiled=True)  43.9 us
    dot_general x26, matrix products, conv_taps(): jnp.einsum('oc,chw->ohw', taps, window, preferred_element_type=jnp.float32)  33.9 us
    scatter-add x1, other arithmetic, on_device(): sums = jax.ops.segment_sum(share.T, mine, num_segments=owners * basins_here)  30.7 us
    dynamic_update_slice x30, other arithmetic, bucket_run(): final, runoff = lax.scan(day, start, (precip, temp, pet))  22.6 us
    sub x30, other arithmetic, day(): lower = lower - base  21.8 us
    all_to_all x1, waiting for transfers between devices, on_device(): lax.all_to_all(sums, 'tile', split_axis=1, concat_axis=1, tiled=True)  12.6 us
    reduce_scatter x1, waiting for transfers between devices, on_device(): lax.psum_scatter(jnp.einsum('cp,chw->hpw', head_weight, hidden, preferred...  12.1 us
    ppermute x3, starting transfers between devices, padded_2(): lax.ppermute(tail, axis, [(i, (i + 1) % count) for i in range(ends)])  10.5 us
  transfers between devices with their start and end apart: 10, of which 7 were waited for; matrix products, arithmetic and copies ran while one was open for 1% of the time, Pallas kernels for 0%

commit v1 on v0

--- a/solution.py
+++ b/solution.py
@@ -117,7 +117,13 @@
     for weight in (conv_second, conv_third):
         rim = padded_2(hidden, (("tile", 1),), 1)
         total = conv_taps(
-            empty, weight, pad_columns(lax.all_gather(rim, "chan", axis=0, tiled=True))
+            empty,
+            weight,
+            pad_columns(
+                jnp.concatenate(
+                    lax.all_to_all(jnp.stack([rim] * lax.axis_size("chan")), "chan", 0, 0), axis=0
+                )
+            ),
         )
         hidden = jnp.maximum(total, 0.0).astype(jnp.bfloat16)
     raw = lax.psum_scatter(

time: 259 us -> 236 us (0.911)
  waiting for transfers between devices: 77.8 us -> 41.6 us
  blocking collectives: 3.81 us -> 19.5 us
  matrix products: 46.1 us -> 42.8 us
    all_gather x2 -> x0, waiting for transfers between devices: 43.9 us -> none  [on_device(): lax.all_gather(rim, 'chan', axis=0, tiled=True)]
    all_to_all x0 -> x2, blocking collectives: none -> 15.7 us  [on_device(): lax.all_to_all(jnp.stack([rim] * lax.axis_size('chan')), 'chan', 0, 0)]
    reduce_scatter x1, waiting for transfers between devices: 12.1 us -> 19.5 us  [on_device(): lax.psum_scatter(jnp.einsum('cp,chw->hpw', head_weight, hidden, preferred...]
    dot_general x26, matrix products: 33.9 us -> 30.5 us  [conv_taps(): jnp.einsum('oc,chw->ohw', taps, window, preferred_element_type=jnp.float32)]
  transfers between devices with their start and end apart: 10 -> 8, of which waited for: 7 -> 5; matrix products, arithmetic and copies ran while one was open for 1% -> 1% of each run, Pallas kernels for 0% -> 0%
where the time goes in v1:
time: 236 us; the launch traced here: 233 us
  other arithmetic  77.6 us (33%)
  matrix products  42.8 us (18%)
  waiting for transfers between devices  41.6 us (18%)
  starting transfers between devices  25.9 us (11%)
  blocking collectives  19.5 us (8%)
  between operations  13.8 us (6%)
  local copies, waits for them, and re-layouts  10.8 us (5%)
    scatter-add x1, other arithmetic, on_device(): sums = jax.ops.segment_sum(share.T, mine, num_segments=owners * basins_here)  30.7 us
    dot_general x26, matrix products, conv_taps(): jnp.einsum('oc,chw->ohw', taps, window, preferred_element_type=jnp.float32)  30.5 us
    dynamic_update_slice x30, other arithmetic, bucket_run(): final, runoff = lax.scan(day, start, (precip, temp, pet))  22.6 us
    sub x30, other arithmetic, day(): lower = lower - base  21.8 us
    reduce_scatter x1, waiting for transfers between devices, on_device(): lax.psum_scatter(jnp.einsum('cp,chw->hpw', head_weight, hidden, preferred...  19.5 us
    all_to_all x2, blocking collectives, on_device(): lax.all_to_all(jnp.stack([rim] * lax.axis_size('chan')), 'chan', 0, 0)  15.7 us
    all_to_all x1, waiting for transfers between devices, on_device(): lax.all_to_all(sums, 'tile', split_axis=1, concat_axis=1, tiled=True)  12.7 us
    ppermute x3, starting transfers between devices, padded_2(): lax.ppermute(tail, axis, [(i, (i + 1) % count) for i in range(ends)])  11.8 us
  transfers between devices with their start and end apart: 8, of which 5 were waited for; matrix products, arithmetic and copies ran while one was open for 1% of the time, Pallas kernels for 0%

profile of v1, /device:TPU:1, one launch (start us, length us, event | category | flops | bytes accessed | tf_op | source)
XLA Modules:
  0.0 232.7 jit_solution(14305704264631995043)
XLA Ops:
  6.5 1.4 copy.83
  7.9 3.9 %collective-permute-start = (bf16[35,1,512]{2,0,1:T(8,128)(2,1)S(1)}, bf16[35,1,512]{2,0,1:T(8,128)(2,1)S(1)}, u32[]{:S(2)}, u32[]{:S(2)}) collective-permute-start(bf16[35,1,512]{2,0,1:T(8,128)(2,1)S(1)} %get-tuple-element.376), channel_id=1, source_target_pairs={{0,2},{2,4},{4,6},{6,8},{8,10},{10,12},{12,14},{14,16},{16,18},{18... | collective-permute-start | bytes 107528 | tf_op jit(solution)/shard_map/ppermute | solution.py:19
  11.9 1.4 collective-permute-start.1
  13.3 1.7 fusion.125
  15.1 1.7 collective-permute-done.1
  20.9 2.4 %fusion.36 = bf16[64,16,512]{2,0,1:T(8,128)(2,1)S(1)} fusion(f32[16,512,64]{1,2,0:T(8,128)S(1)} %fusion.66, f32[16,512,64]{1,2,0:T(8,128)S(1)} %fusion.71, f32[16,512,64]{1,2,0:T(8,128)S(1)} %fusion.73, f32[64,16,512]{2,0,1:T(8,128)S(1)} %fusion.125, f32[16,512,64]{1,2,0:T(8,128)S(1)} %fusion.75, f32[16,512,64]{1,2,0:T(8,128)S(1)} %fusion.77, ...), kind=kOutput, calls=%fused_computation.71 | convolution fusion | flops 41943040 | bytes 18491392 | tf_op jit(solution)/shard_map/oc,chw->ohw/dot_general | solution.py:39
  23.3 3.1 %collective-permute-start.2 = (bf16[64,1,512]{2,0,1:T(8,128)(2,1)S(1)}, bf16[64,1,512]{2,0,1:T(8,128)(2,1)S(1)}, u32[]{:S(2)}, u32[]{:S(2)}) collective-permute-start(bf16[64,1,512]{2,0,1:T(8,128)(2,1)S(1)} %get-tuple-element.374), channel_id=1, source_target_pairs={{0,2},{2,4},{4,6},{6,8},{8,10},{10,12},{12,14},{14,16},{16,18},{18... | collective-permute-start | bytes 196616 | tf_op jit(solution)/shard_map/ppermute | solution.py:19
  26.4 1.3 collective-permute-start.3
  27.7 3.7 %collective-permute-done.3 = bf16[64,1,512]{2,0,1:T(8,128)(2,1)S(1)} collective-permute-done((bf16[64,1,512]{2,0,1:T(8,128)(2,1)S(1)}, bf16[64,1,512]{2,0,1:T(8,128)(2,1)S(1)}, u32[]{:S(2)}, u32[]{:S(2)}) %collective-permute-start.3) | collective-permute-done | bytes 65568 | tf_op jit(solution)/shard_map/ppermute | solution.py:21
  31.8 8.9 %all_to_all.15 = bf16[2,64,18,512]{3,1,2,0:T(8,128)(2,1)S(1)} all-to-all(bf16[2,64,18,512]{3,1,2,0:T(8,128)(2,1)S(1)} %pad_maximum_fusion), channel_id=1, replica_groups=mesh['tile'=64,'chan'=2] {'chan'}, dimensions={0} | all-to-all | bytes 4718592 | tf_op jit(solution)/shard_map/all_to_all | solution.py:124
  40.8 0.8 copy-done.2
  41.6 0.8 fusion.11
  42.4 0.8 fusion.12
  43.1 0.8 fusion.13
  43.9 0.8 fusion.14
  44.7 0.8 fusion.15
  45.5 0.8 fusion.16
  47.2 1.1 fusion.44
  48.3 4.8 %collective-permute-start.4 = (bf16[64,1,512]{2,0,1:T(8,128)(2,1)S(1)}, bf16[64,1,512]{2,0,1:T(8,128)(2,1)S(1)}, u32[]{:S(2)}, u32[]{:S(2)}) collective-permute-start(bf16[64,1,512]{2,0,1:T(8,128)(2,1)S(1)} %get-tuple-element.372), channel_id=1, source_target_pairs={{0,2},{2,4},{4,6},{6,8},{8,10},{10,12},{12,14},{14,16},{16,18},{18... | collective-permute-start | bytes 196616 | tf_op jit(solution)/shard_map/ppermute | solution.py:19
  53.0 1.3 collective-permute-start.5
  54.4 4.0 %collective-permute-done.5 = bf16[64,1,512]{2,0,1:T(8,128)(2,1)S(1)} collective-permute-done((bf16[64,1,512]{2,0,1:T(8,128)(2,1)S(1)}, bf16[64,1,512]{2,0,1:T(8,128)(2,1)S(1)}, u32[]{:S(2)}, u32[]{:S(2)}) %collective-permute-start.5) | collective-permute-done | bytes 65568 | tf_op jit(solution)/shard_map/ppermute | solution.py:21
  58.7 6.8 %all_to_all.16 = bf16[2,64,18,512]{3,1,2,0:T(8,128)(2,1)S(1)} all-to-all(bf16[2,64,18,512]{3,1,2,0:T(8,128)(2,1)S(1)} %pad_maximum_fusion.1), channel_id=1, replica_groups=mesh['tile'=64,'chan'=2] {'chan'}, dimensions={0} | all-to-all | bytes 4718592 | tf_op jit(solution)/shard_map/all_to_all | solution.py:124
  66.4 2.1 fusion.17
  68.5 2.1 fusion.18
  70.6 2.1 fusion.19
  72.7 2.1 fusion.20
  74.9 2.1 fusion.21
  77.0 2.1 fusion.22
  79.1 1.7 fusion.23
  80.8 1.8 fusion.25
  82.6 8.2 %fusion.53 = f32[16,12,512]{2,1,0:T(8,128)} fusion(f32[16,512,64]{1,2,0:T(8,128)} %fusion.22, f32[16,512,64]{1,2,0:T(8,128)} %fusion.23, f32[16,512,64]{1,2,0:T(8,128)} %fusion.21, f32[16,512,64]{1,2,0:T(8,128)} %fusion.20, f32[16,512,64]{1,2,0:T(8,128)} %fusion.25, f32[16,512,64]{1,2,0:T(8,128)} %fusion.19, f32[16,512,64]{1,2,0:T(8,128)} %fusion.18, ...), kind=kOutput, calls=%fused_computation.85 | convolution fusion | flops 152043520 | bytes 19288064 | tf_op jit(solution)/shard_map/cp,chw->hpw/dot_general | solution.py:130
  91.0 19.5 %reduce-scatter.2.cloned.1.call-done = f32[8,12,512]{2,1,0:T(8,128)} async-done(((f32[16,12,512]{2,1,0:T(8,128)}), f32[8,12,512]{2,1,0:T(8,128)}) %reduce-scatter.2.cloned.1.call-update) | async-done | bytes 196624 | tf_op jit(solution)/shard_map/reduce_scatter | solution.py:129
  110.5 1.0 divide_bitcast_fusion
  112.5 30.7 %scatter_custom_fusion = f32[8192,12]{1,0:T(8,128)} fusion(s32[4096]{0:T(1024)S(1)} %bitcast.313, f32[4096,12]{1,0:T(8,128)S(1)} %copy.92, f32[]{:T(128)} %constant.50.clone.1), kind=kCustom, calls=%fused_computation.78 | custom fusion | flops 49152 | bytes 393220 | tf_op jit(solution)/shard_map/scatter-add | solution.py:139
  143.2 3.6 %copy.93 = f32[12,64,128]{2,0,1:T(8,128)} copy(f32[12,64,128]{0,2,1:T(8,128)} %bitcast.293) | data formatting | bytes 786432 | tf_op jit(solution)/shard_map/reshape | solution.py:140
  146.8 10.1 %all-to-all-start.2 = ((f32[12,64,128]{2,0,1:T(8,128)}), f32[12,64,128]{2,0,1:T(8,128)S(1)}, u32[]{:S(2)}, u32[]{:S(2)}) async-start(f32[12,64,128]{2,0,1:T(8,128)} %copy.93), calls=%async_computation.3 | async-start | bytes 1048576 | tf_op jit(solution)/shard_map/all_to_all | solution.py:141
  157.0 12.7 %all-to-all-done.2 = f32[12,64,128]{2,0,1:T(8,128)S(1)} async-done(((f32[12,64,128]{2,0,1:T(8,128)}), f32[12,64,128]{2,0,1:T(8,128)S(1)}, u32[]{:S(2)}, u32[]{:S(2)}) %all-to-all-start.2) | async-done | bytes 393248 | tf_op jit(solution)/shard_map/all_to_all | solution.py:141
  169.8 3.8 %psum.7 = f32[12,128]{1,0:T(8,128)S(1)} all-reduce(f32[12,128]{1,0:T(8,128)S(1)} %reduce_sum.18), channel_id=1, replica_groups=mesh['tile'=64,'chan'=2] {'chan'}, use_global_device_ids=true, to_apply=%region_3.4 | all-reduce | flops 1536 | bytes 12288 | tf_op jit(solution)/shard_map/psum | solution.py:143
  174.4 1.9 copy.97
  176.3 45.1 %while.21 = (s32[]{:T(128)}, f32[8,128]{1,0:T(8,128)S(1)}, f32[8,128]{1,0:T(8,128)S(1)}, f32[8,128]{1,0:T(8,128)S(1)}, f32[8,128]{1,0:T(8,128)S(1)}, /*index=5*/...) while((s32[]{:T(128)}, f32[8,128]{1,0:T(8,128)S(1)}, ...), condition=%wide.region_5.6_spmd.clone, body=%wide.region_4.5_spmd.clone.sunk | while | flops 63491 | bytes 82640 | solution.py:79
  200.3 0.8 fusion.177
  201.8 0.8 fusion.177
  203.3 0.8 fusion.177
  207.8 0.8 fusion.177
  209.4 0.8 fusion.177
  210.9 0.8 fusion.177
  221.6 3.4 %convolution_bitcast_fusion = f32[30,8,128]{0,1,2:T(8,128)S(1)} fusion(f32[30,8,128]{0,1,2:T(8,128)S(1)} %copy.96, f32[30,30,128]{1,0,2:T(8,128)S(1)} %copy.97), kind=kOutput, calls=%fused_computation.84 | convolution fusion | flops 11059200 | bytes 706560 | tf_op jit(solution)/shard_map/tsb,swb->twb/dot_general | solution.py:93
  225.0 0.9 copy.98
  (114 shorter events, 48.7 us)
Async XLA Ops:
  6.5 84.4 %copy-start = (s32[16,512]{1,0:T(8,128)S(1)}, s32[16,512]{1,0:T(8,128)}, u32[]{:S(2)}) copy-start(s32[16,512]{1,0:T(8,128)} %param.15) | copy-start | bytes 98308
  6.5 103.9 %reduce-scatter.2.cloned.1.call-start = ((), (), s32[]{:S(2)}) async-start(), calls=%async_computation.4 | async-start | bytes 786432 | tf_op jit(solution)/shard_map/reduce_scatter | solution.py:129
  7.9 7.1 %collective-permute-start = (bf16[35,1,512]{2,0,1:T(8,128)(2,1)S(1)}, bf16[35,1,512]{2,0,1:T(8,128)(2,1)S(1)}, u32[]{:S(2)}, u32[]{:S(2)}) collective-permute-start(bf16[35,1,512]{2,0,1:T(8,128)(2,1)S(1)} %get-tuple-element.376), channel_id=1, source_target_pairs={{0,2},{2,4},{4,6},{6,8},{8,10},{10,12},{12,14},{14,16},{16,18},{18... | collective-permute-start | bytes 107528 | tf_op jit(solution)/shard_map/ppermute | solution.py:19
  11.9 5.4 %copy-start.3 = (bf16[64,3,3,35]{0,3,2,1:T(8,128)(2,1)S(1)}, bf16[64,3,3,35]{0,3,2,1:T(8,128)(2,1)}, u32[]{:S(2)}) copy-start(bf16[64,3,3,35]{0,3,2,1:T(8,128)(2,1)} %param.17) | copy-start | bytes 120964
  11.9 4.9 %collective-permute-start.1 = (bf16[35,1,512]{2,0,1:T(8,128)(2,1)S(1)}, bf16[35,1,512]{2,0,1:T(8,128)(2,1)S(1)}, u32[]{:S(2)}, u32[]{:S(2)}) collective-permute-start(bf16[35,1,512]{2,0,1:T(8,128)(2,1)S(1)} %get-tuple-element.377), channel_id=1, source_target_pairs={{2,0},{4,2},{6,4},{8,6},{10,8},{12,10},{14,12},{16,14},{18,16},{20... | collective-permute-start | bytes 107528 | tf_op jit(solution)/shard_map/ppermute | solution.py:21
  23.3 4.4 %collective-permute-start.2 = (bf16[64,1,512]{2,0,1:T(8,128)(2,1)S(1)}, bf16[64,1,512]{2,0,1:T(8,128)(2,1)S(1)}, u32[]{:S(2)}, u32[]{:S(2)}) collective-permute-start(bf16[64,1,512]{2,0,1:T(8,128)(2,1)S(1)} %get-tuple-element.374), channel_id=1, source_target_pairs={{0,2},{2,4},{4,6},{6,8},{8,10},{10,12},{12,14},{14,16},{16,18},{18... | collective-permute-start | bytes 196616 | tf_op jit(solution)/shard_map/ppermute | solution.py:19
  26.4 5.0 %collective-permute-start.3 = (bf16[64,1,512]{2,0,1:T(8,128)(2,1)S(1)}, bf16[64,1,512]{2,0,1:T(8,128)(2,1)S(1)}, u32[]{:S(2)}, u32[]{:S(2)}) collective-permute-start(bf16[64,1,512]{2,0,1:T(8,128)(2,1)S(1)} %get-tuple-element.375), channel_id=1, source_target_pairs={{2,0},{4,2},{6,4},{8,6},{10,8},{12,10},{14,12},{16,14},{18,16},{20... | collective-permute-start | bytes 196616 | tf_op jit(solution)/shard_map/ppermute | solution.py:21
  40.7 0.9 copy-start.2
  48.3 6.1 %collective-permute-start.4 = (bf16[64,1,512]{2,0,1:T(8,128)(2,1)S(1)}, bf16[64,1,512]{2,0,1:T(8,128)(2,1)S(1)}, u32[]{:S(2)}, u32[]{:S(2)}) collective-permute-start(bf16[64,1,512]{2,0,1:T(8,128)(2,1)S(1)} %get-tuple-element.372), channel_id=1, source_target_pairs={{0,2},{2,4},{4,6},{6,8},{8,10},{10,12},{12,14},{14,16},{16,18},{18... | collective-permute-start | bytes 196616 | tf_op jit(solution)/shard_map/ppermute | solution.py:19
  53.0 5.3 %collective-permute-start.5 = (bf16[64,1,512]{2,0,1:T(8,128)(2,1)S(1)}, bf16[64,1,512]{2,0,1:T(8,128)(2,1)S(1)}, u32[]{:S(2)}, u32[]{:S(2)}) collective-permute-start(bf16[64,1,512]{2,0,1:T(8,128)(2,1)S(1)} %get-tuple-element.373), channel_id=1, source_target_pairs={{2,0},{4,2},{6,4},{8,6},{10,8},{12,10},{14,12},{16,14},{18,16},{20... | collective-permute-start | bytes 196616 | tf_op jit(solution)/shard_map/ppermute | solution.py:21
  65.5 0.9 copy-start.1
  80.8 1.8 copy-start.4
  143.2 13.8 %copy-start.7 = (s32[128]{0:T(128)S(1)}, s32[128]{0:T(128)}, u32[]{:S(2)}) copy-start(s32[128]{0:T(128)} %param.16) | copy-start | bytes 1540
  143.2 30.3 %copy-start.5 = (f32[12]{0:T(128)S(1)}, f32[12]{0:T(128)}, u32[]{:S(2)}) copy-start(f32[12]{0:T(128)} %constant.60.clone) | copy-start | bytes 148
  143.2 30.4 %copy-start.6 = (f32[12]{0:T(128)S(1)}, f32[12]{0:T(128)}, u32[]{:S(2)}) copy-start(f32[12]{0:T(128)} %constant.61.clone) | copy-start | bytes 148
  146.8 22.9 %all-to-all-start.2 = ((f32[12,64,128]{2,0,1:T(8,128)}), f32[12,64,128]{2,0,1:T(8,128)S(1)}, u32[]{:S(2)}, u32[]{:S(2)}) async-start(f32[12,64,128]{2,0,1:T(8,128)} %copy.93), calls=%async_computation.3 | async-start | bytes 1048576 | tf_op jit(solution)/shard_map/all_to_all | solution.py:141
Sparse Core Ops, SparseCore 0:
  91.0 19.3 reduce-scatter.1
